TPU v7x, 32 devices: a whole 2x2x4 slice. The times are simulated.
32 devices in a mesh: dp: 32 (over z, y, x, core).
Axes of the slice: x: 2, y: 2, z: 4, core: 2. Of those that a mesh axis runs over, the one named last changes fastest.
Arguments:
- tokens: bfloat16 [65536, 768], P('dp'), may hold values from -6 to 6
- params: bfloat16 [2, 3765344], P(None, 'dp')
- segments: int32 [65536], P('dp'), may hold values from -1 to 65535, as said below
- cotangent: bfloat16 [65536, 768], P('dp'), may hold values from -6 to 6
Outputs:
- out_tokens: bfloat16 [65536, 768], P('dp')
- grad_tokens: float32 [65536, 768], P('dp')
- grad_params: float32 [2, 3765344], P(None, 'dp')
Inputs may be any that keep to these rules, and one draw needn't show every extreme that they name: `segments`: within each device's block of 1024 slots (one micro-batch), the slots of one packed sequence stand together and share a number that no other sequence has; numbers never fall within a block; unused slots (-1) all stand at a block's end; some block holds one sequence of all 1024 slots.
All inputs are finite; a program needn't handle non-finite values.
Results may differ from a plain program's by a relative error of at most 0.0087.
Values may be sent and summed in bfloat16 or wider, within the bound.
A program may use at most 576 MiB of HBM per device.

v0:
```python
import math

import jax
import jax.numpy as jnp
from jax import lax
from jax.sharding import PartitionSpec as P

D = 768
INNER = 1536
HEADDIM = 64
STATE = 128
KERNEL = 4
GROUP = 256
MB_TOK = 1024
LAYERS = 2
HEADS = 24
CONVCH = 1792
PROJ = 3352
PARAMS = 3765320


highest = lax.Precision.HIGHEST


def layout_shapes():
    return [
        (D,),
        (D, PROJ),
        (KERNEL, CONVCH),
        (CONVCH,),
        (HEADS,),
        (HEADS,),
        (HEADS,),
        (INNER,),
        (INNER, D),
    ]


def unpack(flat_weights):
    pieces = []
    offset = 0
    for piece_shape in layout_shapes():
        amount = math.prod(piece_shape)
        pieces.append(flat_weights[offset : offset + amount].reshape(piece_shape))
        offset = offset + amount
    return pieces


def rms_scale(values):
    return values * lax.rsqrt(jnp.mean(values * values, axis=-1, keepdims=True) + 1e-05)


def norm_gain(values, gains):
    return rms_scale(values) * gains


def group_step(state_in, block):
    (
        feature_block,
        inject_block,
        readout_block,
        step_block,
        decay_block,
        segment_block,
        before_segment,
    ) = block
    length = segment_block.shape[0]
    cumulated = jnp.cumsum(decay_block, axis=0)
    heads_cumulated = cumulated.T
    spread = heads_cumulated[:, :, None] - heads_cumulated[:, None, :]
    causal = (jnp.arange(length)[:, None] >= jnp.arange(length)[None, :]) & (
        segment_block[:, None] == segment_block[None, :]
    )
    within = jnp.exp(jnp.where(causal[None], spread, -1e30))
    scores = jnp.dot(readout_block, inject_block.T, precision=highest)
    mixing = within * scores[None] * step_block.T[:, None, :]
    inside = jnp.einsum("hts,shp->thp", mixing, feature_block, precision=highest)
    carried = (segment_block == before_segment).astype(jnp.float32)[:, None] * jnp.exp(cumulated)
    outside = (
        jnp.einsum("tn,hpn->thp", readout_block, state_in, precision=highest) * carried[:, :, None]
    )
    final_segment = segment_block[length - 1]
    tail_weight = (
        jnp.exp(cumulated[length - 1][None, :] - cumulated)
        * step_block
        * (segment_block == final_segment).astype(jnp.float32)[:, None]
    )
    kept_share = jnp.exp(cumulated[length - 1]) * (final_segment == before_segment).astype(
        jnp.float32
    )
    fresh_state = jnp.einsum(
        "sh,shp,sn->hpn", tail_weight, feature_block, inject_block, precision=highest
    )
    return (state_in * kept_share[:, None, None] + fresh_state, inside + outside)


def mixer_core(
    projected, conv_weight, conv_bias, step_bias, decay_log, skip_gain, out_gain, segment
):
    length = projected.shape[0]
    gate_part = projected[:, :INNER]
    conv_in = projected[:, INNER : INNER + CONVCH]
    step_raw = projected[:, INNER + CONVCH :]
    prior_segment = jnp.concatenate([jnp.full((KERNEL - 1,), -2, jnp.int32), segment])
    padded = jnp.concatenate([jnp.zeros((KERNEL - 1, CONVCH), jnp.float32), conv_in])
    summed = jnp.zeros_like(conv_in) + conv_bias
    for tap_index in range(KERNEL):
        same_doc = (prior_segment[tap_index : tap_index + length] == segment).astype(jnp.float32)[
            :, None
        ]
        summed = summed + conv_weight[tap_index] * padded[tap_index : tap_index + length] * same_doc
    activated = jax.nn.silu(summed)
    features = activated[:, :INNER]
    inject = activated[:, INNER : INNER + STATE]
    readout = activated[:, INNER + STATE :]
    step_size = jax.nn.softplus(step_raw + step_bias)
    log_decay = -jnp.exp(decay_log) * step_size
    blocks = length // GROUP
    earlier = jnp.concatenate([jnp.full((1,), -2, jnp.int32), segment[:-1]])
    scanned = (
        features.reshape(blocks, GROUP, HEADS, HEADDIM),
        inject.reshape(blocks, GROUP, STATE),
        readout.reshape(blocks, GROUP, STATE),
        step_size.reshape(blocks, GROUP, HEADS),
        log_decay.reshape(blocks, GROUP, HEADS),
        segment.reshape(blocks, GROUP),
        earlier.reshape(blocks, GROUP)[:, 0],
    )
    state_zero = jnp.zeros((HEADS, HEADDIM, STATE), jnp.float32)
    final_state, mixed_heads = lax.scan(jax.checkpoint(group_step), state_zero, scanned)
    mixed_heads = mixed_heads.reshape(length, HEADS, HEADDIM) + skip_gain[
        None, :, None
    ] * features.reshape(length, HEADS, HEADDIM)
    gated = mixed_heads.reshape(length, INNER) * jax.nn.silu(gate_part)
    return rms_scale(gated) * out_gain


def contract_rows(left_side, right_side):
    return lax.dot_general(
        left_side, right_side, (((0,), (0,)), ((), ())), preferred_element_type=jnp.float32
    )


def contract_cols(left_side, right_side):
    return lax.dot_general(
        left_side, right_side, (((1,), (1,)), ((), ())), preferred_element_type=jnp.float32
    )


def flatten_layer(members, padded_total):
    return jnp.concatenate(
        [member.reshape(-1) for member in members]
        + [jnp.zeros((padded_total - PARAMS,), jnp.float32)]
    )


def per_device(tokens, params, segments, cotangent):
    micro_count = tokens.shape[0] // MB_TOK
    padded_total = params.shape[1] * lax.axis_size("dp")
    kept_records = []
    finals = []
    for micro_index in range(micro_count):
        first_row = micro_index * MB_TOK
        segment = segments[first_row : first_row + MB_TOK]
        live_rows = (segment >= 0).astype(jnp.float32)[:, None]
        stream = tokens[first_row : first_row + MB_TOK].astype(jnp.float32)
        records = []
        for layer_index in range(LAYERS):
            flat_weights = lax.all_gather(params[layer_index], "dp", axis=0, tiled=True)
            pieces = unpack(flat_weights)
            normed_value, norm_pull = jax.vjp(norm_gain, stream, pieces[0].astype(jnp.float32))
            normed = normed_value.astype(jnp.bfloat16)
            projected = jnp.dot(normed, pieces[1], preferred_element_type=jnp.float32)
            small_params = tuple((member.astype(jnp.float32) for member in pieces[2:8]))

            def mixer_local(proj_in, *extras):
                return mixer_core(proj_in, *extras, segment)

            mixer_value, mixer_pull = jax.vjp(mixer_local, projected, *small_params)
            mixer_out = mixer_value.astype(jnp.bfloat16)
            stream = (
                stream
                + jnp.dot(mixer_out, pieces[8], preferred_element_type=jnp.float32) * live_rows
            )
            records.append((normed, mixer_out, norm_pull, mixer_pull))
        kept_records.append(records)
        finals.append(stream.astype(jnp.bfloat16))
    totals = [None] * LAYERS
    grad_rows = []
    for micro_index in range(micro_count):
        first_row = micro_index * MB_TOK
        segment = segments[first_row : first_row + MB_TOK]
        live_rows = (segment >= 0).astype(jnp.float32)[:, None]
        grad_stream = cotangent[first_row : first_row + MB_TOK].astype(jnp.float32)
        for layer_index in reversed(range(LAYERS)):
            flat_weights = lax.all_gather(params[layer_index], "dp", axis=0, tiled=True)
            pieces = unpack(flat_weights)
            normed, mixer_out, norm_pull, mixer_pull = kept_records[micro_index][layer_index]
            branch = (grad_stream * live_rows).astype(jnp.bfloat16)
            grad_out_weight = contract_rows(mixer_out, branch)
            grad_mixer = contract_cols(branch, pieces[8])
            mixer_grads = mixer_pull(grad_mixer)
            grad_projected = mixer_grads[0].astype(jnp.bfloat16)
            grad_in_weight = contract_rows(normed, grad_projected)
            grad_normed = contract_cols(grad_projected, pieces[1])
            stream_part, gain_grad = norm_pull(grad_normed)
            grad_stream = grad_stream + stream_part
            layer_grads = [gain_grad, grad_in_weight] + list(mixer_grads[1:]) + [grad_out_weight]
            if totals[layer_index] is None:
                totals[layer_index] = layer_grads
            else:
                totals[layer_index] = [
                    before + after for before, after in zip(totals[layer_index], layer_grads)
                ]
        grad_rows.append(grad_stream)
    flat_grads = jnp.stack(
        [flatten_layer(totals[layer_index], padded_total) for layer_index in range(LAYERS)]
    )
    grad_shards = lax.psum_scatter(flat_grads, "dp", scatter_dimension=1, tiled=True)
    return (jnp.concatenate(finals, axis=0), jnp.concatenate(grad_rows, axis=0), grad_shards)


def solution(mesh):
    in_specs = (P("dp", None), P(None, "dp"), P("dp"), P("dp", None))
    out_specs = (P("dp", None), P("dp", None), P(None, "dp"))
    return jax.shard_map(
        per_device, mesh=mesh, in_specs=in_specs, out_specs=out_specs, check_vma=False
    )
```

profile of v0, /device:TPU:0, one launch (start us, length us, event | category | flops | bytes accessed | tf_op | source)
XLA Modules:
  0.0 5233.1 jit_solution(16146647253494684360)
XLA Ops:
  34.0 255.7 %all-reduce.79.cloned.1.call-done = (bf16[3765344]{0:T(1024)(128)(2,1)}, bf16[3765344]{0:T(1024)(128)(2,1)}) async-done(((bf16[3765344]{0:T(1024)(128)(2,1)}, bf16[3765344]{0:T(1024)(128)(2,1)}), (bf16[3765344]{0:T(1024)(128)(2,1)}, bf16[3765344]{0:T(1024)(128)(2,1)})) %all-reduce.79.cloned.1.call-update) | async-done | bytes 15061392
  289.7 72.8 %reshape.1947 = bf16[1,3765344]{1,0:T(2,128)(2,1)} reshape(bf16[3765344]{0:T(1024)(128)(2,1)} %get-tuple-element.2995) | data formatting | bytes 15061376
  363.2 103.6 %slice_reduce_fusion.21 = bf16[2574336]{0:T(1024)(128)(2,1)} fusion(bf16[1,3765344]{1,0:T(2,128)(2,1)} %reshape.1947), kind=kLoop, calls=%fused_computation.570 | loop fusion | bytes 10297344 | tf_op jit(solution)/shard_map/slice | solution.py:44
  514.9 35.9 fusion.387
  565.5 51.9 slice_reduce_fusion.23
  617.4 86.9 %reshape.1949 = bf16[1,3765344]{1,0:T(2,128)(2,1)} reshape(bf16[3765344]{0:T(1024)(128)(2,1)S(1)} %bitcast.1529) | data formatting | bytes 15061376
  705.1 103.6 %slice_reduce_fusion.20 = bf16[2574336]{0:T(1024)(128)(2,1)} fusion(bf16[1,3765344]{1,0:T(2,128)(2,1)} %reshape.1949), kind=kLoop, calls=%fused_computation.569 | loop fusion | bytes 10297344 | tf_op jit(solution)/shard_map/slice | solution.py:44
  839.8 246.4 %while.166 = (s32[]{:T(128)}, f32[24,64,128]{2,1,0:T(8,128)S(1)}, f32[4,256,24,64]{1,0,3,2:T(4,128)}, f32[4,24,64,128]{3,2,1,0:T(8,128)}, f32[4,256,24]{1,2,0:T(...) while((s32[]{:T(128)}, f32[24,64,128]{2,1,0:T(8,128)S(1)}, ...), condition=%wide.region_16.18_spmd.clone, body=%wide.region_13.17_spmd.clone.sunk | while | flops 2526051328 | bytes 19724684 | solution.py:130
  1117.4 246.7 %while.164 = (s32[]{:T(128)}, f32[24,64,128]{2,1,0:T(8,128)S(1)}, f32[4,256,24,64]{1,0,3,2:T(4,128)}, f32[4,24,64,128]{3,2,1,0:T(8,128)}, f32[4,256,24]{1,2,0:T(...) while((s32[]{:T(128)}, f32[24,64,128]{2,1,0:T(8,128)S(1)}, ...), condition=%wide.region_4.6_spmd.clone, body=%wide.region_1.5_spmd.clone.sunk | while | flops 2526051328 | bytes 19724684 | solution.py:130
  1458.3 34.7 fusion.386
  1505.3 52.1 slice_reduce_fusion.22
  1583.7 246.8 %while.167 = (s32[]{:T(128)}, f32[24,64,128]{2,1,0:T(8,128)S(1)}, f32[4,256,24,64]{1,0,3,2:T(4,128)}, f32[4,24,64,128]{3,2,1,0:T(8,128)}, f32[4,256,24]{1,2,0:T(...) while((s32[]{:T(128)}, f32[24,64,128]{2,1,0:T(8,128)S(1)}, ...), condition=%wide.region_22.24_spmd.clone, body=%wide.region_19.23_spmd.clone.sunk | while | flops 2526051328 | bytes 19724684 | solution.py:130
  1605.8 34.5 dynamic_update_slice.299
  1667.4 34.5 dynamic_update_slice.299
  1729.0 34.5 dynamic_update_slice.299
  1790.6 34.5 dynamic_update_slice.299
  1861.8 247.7 %while.165 = (s32[]{:T(128)}, f32[24,64,128]{2,1,0:T(8,128)S(1)}, f32[4,256,24,64]{1,0,3,2:T(4,128)}, f32[4,24,64,128]{3,2,1,0:T(8,128)}, f32[4,256,24]{1,2,0:T(...) while((s32[]{:T(128)}, f32[24,64,128]{2,1,0:T(8,128)S(1)}, ...), condition=%wide.region_10.12_spmd.clone, body=%wide.region_7.11_spmd.clone.sunk | while | flops 2526051328 | bytes 19724684 | solution.py:130
  1883.6 34.6 dynamic_update_slice.295
  1945.5 34.6 dynamic_update_slice.295
  2007.3 34.6 dynamic_update_slice.295
  2069.1 34.6 dynamic_update_slice.295
  2182.2 408.4 %while.168 = (s32[]{:T(128)}, f32[24,64,128]{2,1,0:T(8,128)}, f32[4,256,24,64]{1,0,3,2:T(4,128)}, f32[4,256,128]{2,1,0:T(8,128)}, f32[4,256,128]{2,1,0:T(8,128)}...) while((s32[]{:T(128)}, f32[24,64,128]{2,1,0:T(8,128)}, ...), condition=%wide.region_37.39_spmd.clone, body=%wide.region_25.38_spmd.clone.sunk | while | flops 5770961920 | bytes 60549120 | solution.py:130
  2253.9 34.7 dynamic_update_slice.302
  2351.6 34.7 dynamic_update_slice.302
  2449.4 34.7 dynamic_update_slice.302
  2547.2 34.7 dynamic_update_slice.302
  2642.3 397.9 %while.170 = (s32[]{:T(128)}, f32[24,64,128]{2,1,0:T(8,128)}, f32[4,256,24,64]{1,0,3,2:T(4,128)}, f32[4,256,128]{2,1,0:T(8,128)}, f32[4,256,128]{2,1,0:T(8,128)}...) while((s32[]{:T(128)}, f32[24,64,128]{2,1,0:T(8,128)}, ...), condition=%wide.region_67.69_spmd.clone, body=%wide.region_55.68_spmd.clone.sunk | while | flops 5770961920 | bytes 60549120 | solution.py:130
  2696.0 34.7 dynamic_update_slice.312
  2793.8 34.7 dynamic_update_slice.312
  2891.6 34.7 dynamic_update_slice.312
  2989.4 34.7 dynamic_update_slice.312
  3245.9 390.6 %while.169 = (s32[]{:T(128)}, f32[24,64,128]{2,1,0:T(8,128)}, f32[4,256,24,64]{1,0,3,2:T(4,128)}, f32[4,256,128]{2,1,0:T(8,128)}, f32[4,256,128]{2,1,0:T(8,128)}...) while((s32[]{:T(128)}, f32[24,64,128]{2,1,0:T(8,128)}, ...), condition=%wide.region_52.54_spmd.clone, body=%wide.region_40.53_spmd.clone.sunk | while | flops 5770961920 | bytes 60549120 | solution.py:130
  3299.7 34.7 dynamic_update_slice.307
  3397.5 34.7 dynamic_update_slice.307
  3495.3 34.7 dynamic_update_slice.307
  3593.1 34.7 dynamic_update_slice.307
  3678.5 397.1 %while.171 = (s32[]{:T(128)}, f32[24,64,128]{2,1,0:T(8,128)}, f32[4,256,24,64]{1,0,3,2:T(4,128)}, f32[4,256,128]{2,1,0:T(8,128)}, f32[4,256,128]{2,1,0:T(8,128)}...) while((s32[]{:T(128)}, f32[24,64,128]{2,1,0:T(8,128)}, ...), condition=%wide.region_82.84_spmd.clone, body=%wide.region_70.83_spmd.clone.sunk | while | flops 5770961920 | bytes 60549120 | solution.py:130
  3732.1 34.7 dynamic_update_slice.317
  3829.7 34.7 dynamic_update_slice.317
  3927.3 34.7 dynamic_update_slice.317
  4024.9 34.7 dynamic_update_slice.317
  4098.6 37.7 multiply_reduce_fusion.26
  4302.0 125.8 %concatenate.50 = f32[3765344]{0:T(1024)} concatenate(f32[768]{0:T(1024)S(1)} %add.613, f32[2574336]{0:T(1024)} %reshape.1876, f32[7168]{0:T(1024)S(1)} %copy-done.127, f32[1792]{0:T(1024)S(1)} %add.616, f32[24]{0:T(128)S(1)} %add.617, f32[24]{0:T(128)S(1)} %add_multiply_fusion.1, f32[24]{0:T(128)S(1)} %add.619, f32[1536]{0:T(1024)S(1)} %add.620, f32[1179648]{0:T(1024)} %reshape.1886, ...), dimensions={0} | concatenate | bytes 30122752 | tf_op jit(solution)/shard_map/concatenate | solution.py:151
  4427.8 57.5 %stack.9 = f32[1,3765344]{1,0:T(1,128)} reshape(f32[3765344]{0:T(1024)} %concatenate.50) | data formatting | bytes 30122752 | tf_op jit(solution)/shard_map/stack | solution.py:216
  4543.7 125.8 %concatenate.51 = f32[3765344]{0:T(1024)} concatenate(f32[768]{0:T(1024)S(1)} %add.622, f32[2574336]{0:T(1024)} %reshape.1887, f32[7168]{0:T(1024)S(1)} %reshape.1896, f32[1792]{0:T(1024)S(1)} %add.625, f32[24]{0:T(128)S(1)} %add.626, f32[24]{0:T(128)S(1)} %add_multiply_fusion, f32[24]{0:T(128)S(1)} %add.628, f32[1536]{0:T(1024)S(1)} %add.629, f32[1179648]{0:T(1024)} %reshape.1897, ...), dimensions={0} | concatenate | bytes 30122752 | tf_op jit(solution)/shard_map/concatenate | solution.py:151
  4669.4 57.3 %stack.10 = f32[1,3765344]{1,0:T(1,128)} reshape(f32[3765344]{0:T(1024)} %concatenate.51) | data formatting | bytes 30122752 | tf_op jit(solution)/shard_map/stack | solution.py:216
  4726.8 42.6 pad_maximum_fusion
  4792.7 430.1 %all-reduce.77.cloned.1.call-done = f32[2,3765344]{1,0:T(2,128)} async-done(((f32[2,3765344]{1,0:T(2,128)}), f32[2,3765344]{1,0:T(2,128)}) %all-reduce.77.cloned.1.call-update) | async-done | bytes 30122768
  (2175 shorter events, 2628.4 us)
Async XLA Ops:
  7.2 282.5 %all-reduce.79.cloned.1.call-start = ((), (), s32[]{:S(2)}) async-start(), calls=%async_computation.1 | async-start | bytes 30130176
  27.3 5195.5 %all-reduce.77.cloned.1.call-start = ((), (), s32[]{:S(2)}) async-start(), calls=%async_computation | async-start | bytes 60246016
  33.2 445.7 %copy-start.200 = (f32[1024]{0:T(1024)}, f32[1024]{0:T(1024)S(1)}, u32[]{:S(2)}) copy-start(f32[1024]{0:T(1024)S(1)} %fusion.470) | copy-start | bytes 12292
  33.2 458.7 %copy-start.202 = (f32[1024]{0:T(1024)}, f32[1024]{0:T(1024)S(1)}, u32[]{:S(2)}) copy-start(f32[1024]{0:T(1024)S(1)} %fusion.466) | copy-start | bytes 12292
  33.9 480.9 %copy-start.87 = (f32[1024]{0:T(1024)}, f32[1024]{0:T(1024)S(1)}, u32[]{:S(2)}) copy-start(f32[1024]{0:T(1024)S(1)} %get-tuple-element.3206) | copy-start | bytes 12292
  33.9 480.9 %copy-start.91 = (f32[1024]{0:T(1024)}, f32[1024]{0:T(1024)S(1)}, u32[]{:S(2)}) copy-start(f32[1024]{0:T(1024)S(1)} %get-tuple-element.3207) | copy-start | bytes 12292
  33.9 480.9 %copy-start.95 = (f32[1024]{0:T(1024)}, f32[1024]{0:T(1024)S(1)}, u32[]{:S(2)}) copy-start(f32[1024]{0:T(1024)S(1)} %get-tuple-element.3208) | copy-start | bytes 12292
  34.0 480.9 %copy-start.99 = (f32[1024]{0:T(1024)}, f32[1024]{0:T(1024)S(1)}, u32[]{:S(2)}) copy-start(f32[1024]{0:T(1024)S(1)} %get-tuple-element.3209) | copy-start | bytes 12292
  34.0 480.9 %copy-start.103 = (f32[1024]{0:T(1024)}, f32[1024]{0:T(1024)S(1)}, u32[]{:S(2)}) copy-start(f32[1024]{0:T(1024)S(1)} %get-tuple-element.3210) | copy-start | bytes 12292
  34.0 480.9 %copy-start.107 = (f32[1024]{0:T(1024)}, f32[1024]{0:T(1024)S(1)}, u32[]{:S(2)}) copy-start(f32[1024]{0:T(1024)S(1)} %get-tuple-element.3211) | copy-start | bytes 12292
  363.2 128.8 %copy-start.195 = (f32[768]{0:T(1024)}, f32[768]{0:T(1024)S(1)}, u32[]{:S(2)}) copy-start(f32[768]{0:T(1024)S(1)} %fusion.475) | copy-start | bytes 9220
  552.2 65.2 %slice-start.14 = ((s8[7532544]{0:T(1024)(128)(4,1)}), s8[4194304]{0:T(1024)(128)(4,1)S(1)}, s32[]{:S(2)}) async-start(s8[7532544]{0:T(1024)(128)(4,1)} %bitcast.1528), calls=%async_computation.16 | async-start | bytes 8388608
  559.6 271.6 %copy-start.214 = (f32[24]{0:T(128)}, f32[24]{0:T(128)S(1)}, u32[]{:S(2)}) copy-start(f32[24]{0:T(128)S(1)} %get-tuple-element.3146) | copy-start | bytes 292
  560.3 270.9 %copy-start.230 = (f32[24]{0:T(128)}, f32[24]{0:T(128)S(1)}, u32[]{:S(2)}) copy-start(f32[24]{0:T(128)S(1)} %fusion.484) | copy-start | bytes 292
  561.4 56.0 %slice-start.15 = ((s8[7532544]{0:T(1024)(128)(4,1)}), s8[3338240]{0:T(1024)(128)(4,1)S(1)}, s32[]{:S(2)}) async-start(s8[7532544]{0:T(1024)(128)(4,1)} %bitcast.1528), calls=%async_computation.17 | async-start | bytes 6676480
  565.4 869.7 %copy-start.165 = (f32[1536]{0:T(1024)}, f32[1536]{0:T(1024)S(1)}, u32[]{:S(2)}) copy-start(f32[1536]{0:T(1024)S(1)} %fusion.453) | copy-start | bytes 18436
  705.1 737.7 %copy-start.197 = (f32[768]{0:T(1024)}, f32[768]{0:T(1024)S(1)}, u32[]{:S(2)}) copy-start(f32[768]{0:T(1024)S(1)} %fusion.474) | copy-start | bytes 9220
  832.4 277.6 %copy-start.51 = (f32[1024,24]{0,1:T(8,128)}, f32[1024,24]{0,1:T(8,128)S(1)}, u32[]{:S(2)}) copy-start(f32[1024,24]{0,1:T(8,128)S(1)} %get-tuple-element.3030) | copy-start | bytes 294916
  1391.5 43.6 copy-start.158
  1505.3 637.9 %copy-start.137 = (f32[1536]{0:T(1024)}, f32[1536]{0:T(1024)S(1)}, u32[]{:S(2)}) copy-start(f32[1536]{0:T(1024)S(1)} %fusion.452) | copy-start | bytes 18436
  2245.5 47.4 copy-start.117
  2343.3 47.4 copy-start.117
  2441.0 47.4 copy-start.117
  2538.8 47.4 copy-start.117
  2687.7 47.4 copy-start.120
  2785.5 47.4 copy-start.120
  2883.3 47.4 copy-start.120
  2981.1 47.4 copy-start.120
  3155.8 52.2 copy-start.20
  3291.4 47.4 copy-start.123
  3389.2 47.4 copy-start.123
  3487.0 47.4 copy-start.123
  3584.8 47.4 copy-start.123
  3723.7 47.4 copy-start.126
  3821.3 47.4 copy-start.126
  3919.0 47.4 copy-start.126
  4016.6 47.4 copy-start.126
  4087.7 48.6 slice-start.6
  4098.5 37.8 slice-start.7
  4098.5 37.8 copy-start.33
  4098.6 37.8 copy-start.34
  4098.6 37.8 copy-start.102
  4098.6 37.8 copy-start.106
  4098.6 37.8 copy-start.110
  4427.8 57.5 %copy-start.25 = (bf16[2048,768]{1,0:T(8,128)(2,1)S(1)}, bf16[2048,768]{1,0:T(8,128)(2,1)}, u32[]{:S(2)}) copy-start(bf16[2048,768]{1,0:T(8,128)(2,1)} %param.24) | copy-start | bytes 9437188
  4427.8 57.5 %copy-start.140 = (f32[1536]{0:T(1024)S(1)}, f32[1536]{0:T(1024)}, u32[]{:S(2)}) copy-start(f32[1536]{0:T(1024)} %copy-done.137) | copy-start | bytes 18436
  4427.8 57.5 %copy-start.187 = (f32[1024]{0:T(1024)S(1)}, f32[1024]{0:T(1024)}, u32[]{:S(2)}) copy-start(f32[1024]{0:T(1024)} %copy-done.186) | copy-start | bytes 12292
  4427.8 57.5 %copy-start.226 = (f32[1024]{0:T(1024)S(1)}, f32[1024]{0:T(1024)}, u32[]{:S(2)}) copy-start(f32[1024]{0:T(1024)} %get-tuple-element.3203) | copy-start | bytes 12292
  (369 other events, 4199.8 us)
Sparse Core Ops, SparseCore 0:
  27.4 262.2 all-reduce.78
  4769.6 453.1 all-reduce.76
where the time goes:
time: 5300 us; the launch traced here: 5230 us
  local copies, waits for them, and re-layouts  2780 us (52%)
  matrix products  1040 us (20%)
  waiting for transfers between devices  686 us (13%)
  other arithmetic  637 us (12%)
  loops' own time  81.8 us (2%)
    dynamic_update_slice x128, local copies, waits for them, and re-layouts, mixer_core(): lax.scan(jax.checkpoint(group_step), state_zero, scanned)  1230 us
    unnamed x4, waiting for transfers between devices  686 us
    dot_general x48, matrix products, group_step(): jnp.einsum('hts,shp->thp', mixing, feature_block, precision=highest)  406 us
    slice x4, local copies, waits for them, and re-layouts, unpack(): pieces.append(flat_weights[offset:offset + amount].reshape(piece_shape))  311 us
    unnamed x449, local copies, waits for them, and re-layouts  286 us
    concatenate x2, local copies, waits for them, and re-layouts, flatten_layer(): jnp.concatenate([member.reshape(-1) for member in members] + [jnp.zeros((...  252 us
    dot_general x48, matrix products, group_step(): jnp.einsum('sh,shp,sn->hpn', tail_weight, feature_block, inject_block, pr...  155 us
    dot_general x64, matrix products, group_step(): jnp.einsum('tn,hpn->thp', readout_block, state_in, precision=highest)  138 us
  transfers between devices with their start and end apart: 2, of which 2 were waited for; matrix products, arithmetic and copies ran while one was open for 1% of the time, Pallas kernels for 0%

commit v1 on v0

v1 whole, which is shorter than its diff:
```python
import math

import jax
import jax.numpy as jnp
from jax import lax
from jax.experimental import pallas as pl
from jax.experimental.pallas import tpu as pltpu
from jax.sharding import PartitionSpec as P

D = 768
INNER = 1536
HEADDIM = 64
STATE = 128
KERNEL = 4
MB_TOK = 1024
LAYERS = 2
HEADS = 24
CONVCH = 1792
PROJ = 3352
PARAMS = 3765320

LANES = 128
CHUNK = 128
CHUNKS = MB_TOK // CHUNK
PAIRS = HEADS // 2
PROJ_PAD = INNER + CONVCH + LANES
STEP_AT = INNER + CONVCH
TILES = CONVCH // LANES
EDGE = 8
F32 = jnp.float32
BF16 = jnp.bfloat16
highest = lax.Precision.HIGHEST


def tile(index):
    return slice(index * LANES, (index + 1) * LANES)


def dot(left, right, left_dim=1, right_dim=0):
    return lax.dot_general(
        left, right, (((left_dim,), (right_dim,)), ((), ())), preferred_element_type=F32
    )


def exact_dot(left, right):
    return jnp.dot(left, right, preferred_element_type=F32, precision=highest)


def sigmoid(values):
    return 1.0 / (1.0 + jnp.exp(-values))


def softplus(values):
    return jnp.maximum(values, 0.0) + jnp.log1p(jnp.exp(-jnp.abs(values)))


def halves(first, second):
    lane = lax.broadcasted_iota(jnp.int32, (1, LANES), 1)
    return jnp.where(lane < HEADDIM, first, second)


def spread_column(values, index):
    return jnp.broadcast_to(values[:, index : index + 1], (CHUNK, LANES))


def conv_tile(proj_ref, shift_ref, conv_ref, mask, index):
    at = slice(INNER + index * LANES, INNER + (index + 1) * LANES)
    lanes = tile(index)
    total = conv_ref[4:5, lanes] + conv_ref[3:4, lanes] * proj_ref[:, at]
    for back in range(1, KERNEL):
        shifted = shift_ref[EDGE - back : EDGE - back + CHUNK, lanes]
        total = total + conv_ref[3 - back : 4 - back, lanes] * shifted * mask[:, back - 1 : back]
    return total


def load_shift(proj_ref, prev_ref, shift_ref):
    shift_ref[0:EDGE, :] = prev_ref[:, INNER:STEP_AT]
    shift_ref[EDGE : EDGE + CHUNK, :] = proj_ref[:, INNER:STEP_AT]


def decays(proj_ref, head_ref):
    raw = proj_ref[:, STEP_AT:PROJ_PAD] + head_ref[0:1, :]
    step = softplus(raw)
    log_decay = -head_ref[1:2, :] * step
    rows = lax.broadcasted_iota(jnp.int32, (CHUNK, CHUNK), 0)
    cols = lax.broadcasted_iota(jnp.int32, (CHUNK, CHUNK), 1)
    lower = (rows >= cols).astype(F32)
    cumulated = exact_dot(lower, log_decay)
    return raw, step, log_decay, cumulated, rows, cols


def pair_decay(cumulated, turned, bias_twice, first):
    wide_a = spread_column(cumulated, first)
    wide_b = spread_column(cumulated, first + 1)
    row = jnp.concatenate([turned[first : first + 1, :], turned[first + 1 : first + 2, :]], axis=1)
    within = jnp.exp(jnp.concatenate([wide_a, wide_b], axis=1) - row + bias_twice)
    return within, halves(wide_a, wide_b)


def stack_pair(values):
    zero = jnp.zeros_like(values)
    return jnp.concatenate([halves(values, zero), halves(zero, values)], axis=0)


def pair_row(row, first):
    return halves(row[:, first : first + 1], row[:, first + 1 : first + 2])


def forward_kernel(
    proj_ref, prev_ref, mask_ref, seg_col_ref, seg_row_ref, conv_ref, head_ref, wide_ref,
    out_ref, mixed_ref, kept_ref, state_ref, shift_ref, gated_ref,
):
    @pl.when(pl.program_id(1) == 0)
    def _():
        state_ref[...] = jnp.zeros_like(state_ref)

    load_shift(proj_ref, prev_ref, shift_ref)
    mask = mask_ref[...]
    raw, step, log_decay, cumulated, rows, cols = decays(proj_ref, head_ref)
    turned = cumulated.T
    last = cumulated[CHUNK - 1 : CHUNK, :]
    keep_row = jnp.exp(last) * mask[CHUNK - 1 : CHUNK, 5:6]
    same = (rows >= cols) & (seg_col_ref[...] == seg_row_ref[0])
    bias = jnp.where(same, 0.0, -1e30)
    bias_twice = jnp.concatenate([bias, bias], axis=1)
    summed = conv_tile(proj_ref, shift_ref, conv_ref, mask, PAIRS)
    inject = (summed * sigmoid(summed)).astype(BF16)
    summed = conv_tile(proj_ref, shift_ref, conv_ref, mask, PAIRS + 1)
    readout = (summed * sigmoid(summed)).astype(BF16)
    scores = dot(readout, inject, 1, 1)
    scores_twice = jnp.concatenate([scores, scores], axis=1)
    square = jnp.zeros((CHUNK, 1), F32)
    for pair in range(PAIRS):
        first = 2 * pair
        lanes = tile(pair)
        summed = conv_tile(proj_ref, shift_ref, conv_ref, mask, pair)
        feature = summed * sigmoid(summed)
        stepped = feature * halves(spread_column(step, first), spread_column(step, first + 1))
        within, wide = pair_decay(cumulated, turned, bias_twice, first)
        mixing = (within * scores_twice).astype(BF16)
        mixed = dot(mixing, stack_pair(stepped.astype(BF16)))
        state = state_ref[:, lanes]
        state_low = state.astype(BF16)
        kept_ref[0, :, lanes] = state_low
        mixed = mixed + dot(readout, state_low) * (jnp.exp(wide) * mask[:, 3:4])
        tail = jnp.exp(pair_row(last, first) - wide) * mask[:, 4:5]
        state_ref[:, lanes] = state * pair_row(keep_row, first) + dot(
            inject, (stepped * tail).astype(BF16), 0, 0
        )
        mixed = mixed + wide_ref[0:1, lanes] * feature
        mixed_ref[:, lanes] = mixed
        gate = proj_ref[:, lanes]
        gated = mixed * (gate * sigmoid(gate))
        gated_ref[:, lanes] = gated
        square = square + jnp.sum(gated * gated, axis=1, keepdims=True)
    scale = lax.rsqrt(square * (1.0 / INNER) + 1e-05)
    for pair in range(PAIRS):
        lanes = tile(pair)
        out_ref[:, lanes] = (gated_ref[:, lanes] * scale * wide_ref[1:2, lanes]).astype(BF16)


def backward_kernel(
    proj_ref, prev_ref, mask_ref, seg_col_ref, seg_row_ref, conv_ref, head_ref, wide_ref,
    mixed_ref, kept_ref, grad_ref,
    gproj_ref, gconv_ref, gwide_ref, ghead_ref,
    dstate_ref, shift_ref, carry_ref, back_ref,
):
    @pl.when((pl.program_id(0) == 0) & (pl.program_id(1) == 0))
    def _():
        gconv_ref[...] = jnp.zeros_like(gconv_ref)
        gwide_ref[...] = jnp.zeros_like(gwide_ref)
        ghead_ref[...] = jnp.zeros_like(ghead_ref)

    @pl.when(pl.program_id(1) == 0)
    def _():
        dstate_ref[...] = jnp.zeros_like(dstate_ref)
        carry_ref[...] = jnp.zeros_like(carry_ref)

    load_shift(proj_ref, prev_ref, shift_ref)
    mask = mask_ref[...]
    raw, step, log_decay, cumulated, rows, cols = decays(proj_ref, head_ref)
    turned = cumulated.T
    last = cumulated[CHUNK - 1 : CHUNK, :]
    keep_row = jnp.exp(last) * mask[CHUNK - 1 : CHUNK, 5:6]
    same = (rows >= cols) & (seg_col_ref[...] == seg_row_ref[0])
    bias = jnp.where(same, 0.0, -1e30)
    bias_twice = jnp.concatenate([bias, bias], axis=1)
    summed_inject = conv_tile(proj_ref, shift_ref, conv_ref, mask, PAIRS)
    inject = (summed_inject * sigmoid(summed_inject)).astype(BF16)
    summed_readout = conv_tile(proj_ref, shift_ref, conv_ref, mask, PAIRS + 1)
    readout = (summed_readout * sigmoid(summed_readout)).astype(BF16)
    scores = dot(readout, inject, 1, 1)
    scores_twice = jnp.concatenate([scores, scores], axis=1)

    square = jnp.zeros((CHUNK, 1), F32)
    along = jnp.zeros((CHUNK, 1), F32)
    for pair in range(PAIRS):
        lanes = tile(pair)
        gate = proj_ref[:, lanes]
        gated = mixed_ref[:, lanes] * (gate * sigmoid(gate))
        square = square + jnp.sum(gated * gated, axis=1, keepdims=True)
        along = along + jnp.sum(
            gated * grad_ref[:, lanes] * wide_ref[1:2, lanes], axis=1, keepdims=True
        )
    scale = lax.rsqrt(square * (1.0 / INNER) + 1e-05)
    pull = scale * scale * scale * along * (1.0 / INNER)

    pair_at = lax.broadcasted_iota(jnp.int32, (LANES, LANES), 0) // HEADDIM
    head_at = lax.broadcasted_iota(jnp.int32, (LANES, LANES), 1)
    grad_scores = jnp.zeros((CHUNK, 2 * CHUNK), F32)
    grad_inject = jnp.zeros((CHUNK, STATE), F32)
    grad_readout = jnp.zeros((CHUNK, STATE), F32)
    grad_cumulated = jnp.zeros((CHUNK, LANES), F32)
    grad_step = jnp.zeros((CHUNK, LANES), F32)
    grad_last = jnp.zeros((8, LANES), F32)

    def to_summed(grad_active, summed):
        slope = sigmoid(summed)
        return grad_active * (slope * (1.0 + summed * (1.0 - slope)))

    def conv_back(index, grad_summed):
        lanes = tile(index)
        at = slice(INNER + index * LANES, INNER + (index + 1) * LANES)
        gconv_ref[4:5, lanes] += jnp.sum(grad_summed, axis=0, keepdims=True)
        gconv_ref[3:4, lanes] += jnp.sum(grad_summed * proj_ref[:, at], axis=0, keepdims=True)
        total = conv_ref[3:4, lanes] * grad_summed
        for back in range(1, KERNEL):
            masked = grad_summed * mask[:, back - 1 : back]
            shifted = shift_ref[EDGE - back : EDGE - back + CHUNK, lanes]
            gconv_ref[3 - back : 4 - back, lanes] += jnp.sum(
                masked * shifted, axis=0, keepdims=True
            )
            slot = (index % 2) * (KERNEL - 1) + back - 1
            back_ref[slot, 0:CHUNK, :] = masked
            back_ref[slot, CHUNK : CHUNK + EDGE, :] = carry_ref[back - 1, :, lanes]
            carry_ref[back - 1, :, lanes] = masked[0:EDGE, :]
            total = total + conv_ref[3 - back : 4 - back, lanes] * (
                back_ref[slot, back : back + CHUNK, :]
            )
        gproj_ref[:, at] = total.astype(BF16)

    for pair in range(PAIRS):
        first = 2 * pair
        lanes = tile(pair)
        gather = (head_at == pair_at + first).astype(BF16)
        gate = proj_ref[:, lanes]
        slope = sigmoid(gate)
        silu_gate = gate * slope
        mixed = mixed_ref[:, lanes]
        gated = mixed * silu_gate
        grad_out = grad_ref[:, lanes]
        gwide_ref[1:2, lanes] += jnp.sum(grad_out * gated * scale, axis=0, keepdims=True)
        grad_gated = grad_out * wide_ref[1:2, lanes] * scale - gated * pull
        gproj_ref[:, lanes] = (
            grad_gated * mixed * (slope * (1.0 + gate * (1.0 - slope)))
        ).astype(BF16)
        grad_mixed = grad_gated * silu_gate

        summed = conv_tile(proj_ref, shift_ref, conv_ref, mask, pair)
        feature = summed * sigmoid(summed)
        gwide_ref[0:1, lanes] += jnp.sum(grad_mixed * feature, axis=0, keepdims=True)
        wide_step = halves(spread_column(step, first), spread_column(step, first + 1))
        stepped = feature * wide_step
        stepped_low = stepped.astype(BF16)
        stacked = stack_pair(stepped_low)
        within, wide = pair_decay(cumulated, turned, bias_twice, first)
        mixing = (within * scores_twice).astype(BF16)
        grad_low = grad_mixed.astype(BF16)
        both = dot(mixing, grad_low, 0, 0)
        grad_stepped = halves(both[0:CHUNK, :], both[CHUNK : 2 * CHUNK, :])
        grad_scores = grad_scores + dot(grad_low, stacked, 1, 1) * within
        state_low = kept_ref[0, :, lanes]
        carried = (grad_mixed * (jnp.exp(wide) * mask[:, 3:4])).astype(BF16)
        grad_readout = grad_readout + dot(carried, state_low, 1, 1)
        dstate = dstate_ref[:, lanes]
        dstate_low = dstate.astype(BF16)
        tail = jnp.exp(pair_row(last, first) - wide) * mask[:, 4:5]
        grad_tail = dot(inject, dstate_low) * tail
        grad_inject = grad_inject + dot((stepped * tail).astype(BF16), dstate_low, 1, 1)
        kept_dstate = dstate * pair_row(keep_row, first)
        dstate_ref[:, lanes] = kept_dstate + dot(readout, carried, 0, 0)
        tail_sum = jnp.sum(stepped * grad_tail, axis=0, keepdims=True) + jnp.sum(
            kept_dstate * state_low.astype(F32), axis=0, keepdims=True
        )
        tail_sum = jnp.broadcast_to(tail_sum, (8, LANES))
        tail_high = tail_sum.astype(BF16)
        tail_rest = (tail_sum - tail_high.astype(F32)).astype(BF16)
        grad_last = grad_last + dot(tail_high, gather) + dot(tail_rest, gather)
        flow = (
            grad_low.astype(F32) * (mixed - wide_ref[0:1, lanes] * feature)
            - stepped_low.astype(F32) * grad_stepped
            - stepped * grad_tail
        )
        flow_high = flow.astype(BF16)
        flow_rest = (flow - flow_high.astype(F32)).astype(BF16)
        grad_cumulated = grad_cumulated + dot(
            jnp.concatenate([flow_high, flow_rest], axis=1),
            jnp.concatenate([gather, gather], axis=0),
        )
        grad_stepped = grad_stepped + grad_tail
        grad_step = grad_step + dot((grad_stepped * feature).astype(BF16), gather)
        grad_feature = grad_stepped * wide_step + wide_ref[0:1, lanes] * grad_mixed
        conv_back(pair, to_summed(grad_feature, summed))

    grad_scores = (grad_scores[:, 0:CHUNK] + grad_scores[:, CHUNK : 2 * CHUNK]).astype(BF16)
    grad_readout = grad_readout + dot(grad_scores, inject)
    grad_inject = grad_inject + dot(grad_scores, readout, 0, 0)
    conv_back(PAIRS, to_summed(grad_inject, summed_inject))
    conv_back(PAIRS + 1, to_summed(grad_readout, summed_readout))

    upper = (rows <= cols).astype(F32)
    grad_log = exact_dot(upper, grad_cumulated) + grad_last[0:1, :]
    grad_step = grad_step - head_ref[1:2, :] * grad_log
    lane = lax.broadcasted_iota(jnp.int32, (1, LANES), 1)
    grad_raw = jnp.where(lane < HEADS, grad_step * sigmoid(raw), 0.0)
    gproj_ref[:, STEP_AT:PROJ_PAD] = grad_raw.astype(BF16)
    ghead_ref[0:1, :] += jnp.sum(grad_raw, axis=0, keepdims=True)
    ghead_ref[1:2, :] += jnp.sum(grad_log * log_decay, axis=0, keepdims=True)


def row_specs(order):
    def block(width):
        return pl.BlockSpec((CHUNK, width), lambda m, c: (order(m, c), 0))

    def whole(rows, width):
        return pl.BlockSpec((rows, width), lambda m, c: (0, 0))

    per_edge = CHUNK // EDGE
    common = [
        block(PROJ_PAD),
        pl.BlockSpec(
            (EDGE, PROJ_PAD), lambda m, c: (jnp.maximum(order(m, c) * per_edge - 1, 0), 0)
        ),
        block(8),
        block(1),
        pl.BlockSpec((1, 1, CHUNK), lambda m, c: (order(m, c), 0, 0)),
        whole(8, CONVCH),
        whole(8, LANES),
        whole(8, INNER),
    ]
    state = pl.BlockSpec((1, STATE, INNER), lambda m, c: (order(m, c), 0, 0))
    return common, block, whole, state


def mixer_forward(operands):
    count = operands[0].shape[0]
    common, block, whole, state = row_specs(lambda m, c: m * CHUNKS + c)
    return pl.pallas_call(
        forward_kernel,
        grid=(count // MB_TOK, CHUNKS),
        in_specs=common,
        out_specs=[block(INNER), block(INNER), state],
        out_shape=[
            jax.ShapeDtypeStruct((count, INNER), BF16),
            jax.ShapeDtypeStruct((count, INNER), F32),
            jax.ShapeDtypeStruct((count // CHUNK, STATE, INNER), BF16),
        ],
        scratch_shapes=[
            pltpu.VMEM((STATE, INNER), F32),
            pltpu.VMEM((EDGE + CHUNK, CONVCH), F32),
            pltpu.VMEM((CHUNK, INNER), F32),
        ],
        compiler_params=pltpu.CompilerParams(vmem_limit_bytes=48 * 1024 * 1024),
        cost_estimate=pl.CostEstimate(
            flops=count * INNER * 2000, bytes_accessed=count * INNER * 20, transcendentals=0
        ),
        name="mixer_forward",
    )(*operands)


def mixer_backward(operands, mixed, kept, grad_mixer):
    count = operands[0].shape[0]
    common, block, whole, state = row_specs(lambda m, c: m * CHUNKS + CHUNKS - 1 - c)
    return pl.pallas_call(
        backward_kernel,
        grid=(count // MB_TOK, CHUNKS),
        in_specs=common + [block(INNER), state, block(INNER)],
        out_specs=[block(PROJ_PAD), whole(8, CONVCH), whole(8, INNER), whole(8, LANES)],
        out_shape=[
            jax.ShapeDtypeStruct((count, PROJ_PAD), BF16),
            jax.ShapeDtypeStruct((8, CONVCH), F32),
            jax.ShapeDtypeStruct((8, INNER), F32),
            jax.ShapeDtypeStruct((8, LANES), F32),
        ],
        scratch_shapes=[
            pltpu.VMEM((STATE, INNER), F32),
            pltpu.VMEM((EDGE + CHUNK, CONVCH), F32),
            pltpu.VMEM((KERNEL - 1, EDGE, CONVCH), F32),
            pltpu.VMEM((2 * (KERNEL - 1), CHUNK + EDGE, LANES), F32),
        ],
        compiler_params=pltpu.CompilerParams(vmem_limit_bytes=48 * 1024 * 1024),
        cost_estimate=pl.CostEstimate(
            flops=count * INNER * 6000, bytes_accessed=count * INNER * 30, transcendentals=0
        ),
        name="mixer_backward",
    )(*operands, mixed, kept, grad_mixer)


def segment_masks(segments):
    blocks = segments.reshape(-1, MB_TOK)
    columns = []
    for back in range(1, KERNEL):
        prior = jnp.pad(blocks, ((0, 0), (back, 0)), constant_values=-2)[:, :MB_TOK]
        columns.append((prior == blocks).reshape(-1))
    chunks = blocks.reshape(-1, CHUNKS, CHUNK)
    final = chunks[:, :, CHUNK - 1]
    before = jnp.pad(final, ((0, 0), (1, 0)), constant_values=-2)[:, :CHUNKS]
    columns.append((chunks == before[:, :, None]).reshape(-1))
    columns.append((chunks == final[:, :, None]).reshape(-1))
    columns.append(jnp.broadcast_to((final == before)[:, :, None], chunks.shape).reshape(-1))
    columns.extend([jnp.zeros_like(columns[0])] * 2)
    return jnp.stack(columns, axis=1).astype(F32)


def layout_shapes():
    return [
        (D,),
        (D, PROJ),
        (KERNEL, CONVCH),
        (CONVCH,),
        (HEADS,),
        (HEADS,),
        (HEADS,),
        (INNER,),
        (INNER, D),
    ]


def unpack(flat_weights):
    pieces = []
    offset = 0
    for piece_shape in layout_shapes():
        amount = math.prod(piece_shape)
        pieces.append(flat_weights[offset : offset + amount].reshape(piece_shape))
        offset = offset + amount
    return pieces


def rms_scale(values):
    return values * lax.rsqrt(jnp.mean(values * values, axis=-1, keepdims=True) + 1e-05)


def norm_gain(values, gains):
    return rms_scale(values) * gains


def layer_weights(flat_weights):
    pieces = unpack(flat_weights)
    in_weight = jnp.pad(pieces[1], ((0, 0), (0, PROJ_PAD - PROJ)))
    small = [piece.astype(F32) for piece in pieces[2:8]]
    conv = jnp.concatenate([small[0], small[1][None], jnp.zeros((3, CONVCH), F32)])
    head = jnp.pad(
        jnp.stack([small[2], jnp.exp(small[3])]), ((0, 6), (0, LANES - HEADS))
    )
    wide = jnp.concatenate(
        [jnp.repeat(small[4], HEADDIM)[None], small[5][None], jnp.zeros((6, INNER), F32)]
    )
    return pieces[0].astype(F32), in_weight, (conv, head, wide), pieces[8]


def per_device(tokens, params, segments, cotangent):
    count = tokens.shape[0]
    devices = lax.axis_size("dp")
    shard = params.shape[1]
    padded_shard = -(-shard // 2048) * 2048
    live = (segments >= 0).astype(F32)[:, None]
    masks = segment_masks(segments)
    seg_col = segments[:, None]
    seg_row = segments.reshape(-1, 1, CHUNK)
    weights = []
    for layer in range(LAYERS):
        mine = jnp.pad(params[layer], (0, padded_shard - shard))
        flat = lax.all_gather(mine, "dp", axis=0)[:, :shard].reshape(-1)
        weights.append(layer_weights(flat))
    stream = tokens.astype(F32)
    records = []
    for layer in range(LAYERS):
        in_gain, in_weight, small, out_weight = weights[layer]
        normed_value, norm_pull = jax.vjp(norm_gain, stream, in_gain)
        normed = normed_value.astype(BF16)
        projected = dot(normed, in_weight)
        operands = (projected, projected, masks, seg_col, seg_row) + small
        mixer_out, mixed, kept = mixer_forward(operands)
        stream = stream + dot(mixer_out, out_weight) * live
        records.append((normed, norm_pull, operands, mixer_out, mixed, kept))
    out_tokens = stream.astype(BF16)
    grad_stream = cotangent.astype(F32)
    shards = [None] * LAYERS
    for layer in reversed(range(LAYERS)):
        in_gain, in_weight, small, out_weight = weights[layer]
        normed, norm_pull, operands, mixer_out, mixed, kept = records[layer]
        branch = (grad_stream * live).astype(BF16)
        grad_out_weight = dot(mixer_out, branch, 0, 0)
        grad_mixer = dot(branch, out_weight, 1, 1)
        grad_projected, gconv, gwide, ghead = mixer_backward(operands, mixed, kept, grad_mixer)
        grad_in_weight = dot(normed, grad_projected, 0, 0)[:, :PROJ]
        grad_normed = dot(grad_projected, in_weight, 1, 1)
        stream_part, gain_grad = norm_pull(grad_normed)
        grad_stream = grad_stream + stream_part
        members = [
            gain_grad,
            grad_in_weight,
            gconv[:4],
            gconv[4],
            ghead[0, :HEADS],
            ghead[1, :HEADS],
            gwide[0].reshape(HEADS, HEADDIM).sum(axis=1),
            gwide[1],
            grad_out_weight,
            jnp.zeros((shard * devices - PARAMS,), F32),
        ]
        flat = jnp.concatenate([member.reshape(-1) for member in members])
        rows = jnp.pad(flat.reshape(devices, shard), ((0, 0), (0, padded_shard - shard)))
        rows = rows.reshape(-1, LANES)
        if layer + 1 < LAYERS:
            rows, shards[layer + 1] = lax.optimization_barrier((rows, shards[layer + 1]))
        summed = lax.psum_scatter(rows, "dp", scatter_dimension=0, tiled=True)
        shards[layer] = summed.reshape(-1)[:shard]
    return out_tokens, grad_stream, jnp.stack(shards)


def solution(mesh):
    in_specs = (P("dp", None), P(None, "dp"), P("dp"), P("dp", None))
    out_specs = (P("dp", None), P("dp", None), P(None, "dp"))
    return jax.shard_map(
        per_device, mesh=mesh, in_specs=in_specs, out_specs=out_specs, check_vma=False
    )
```

time: 5300 us -> 1320 us (0.25)
  local copies, waits for them, and re-layouts: 2780 us -> 516 us
  matrix products: 1040 us -> 171 us
  other arithmetic: 637 us -> 27.9 us
  waiting for transfers between devices: 686 us -> 241 us
  Pallas kernels: 0 us -> 323 us
  loops' own time: 81.8 us -> 0 us
    dynamic_update_slice x128 -> x0, local copies, waits for them, and re-layouts: 1230 us -> none  [mixer_core(): lax.scan(jax.checkpoint(group_step), state_zero, scanned)]
    dot_general x248 -> x10, matrix products: 1040 us -> 136 us  [dot(): lax.dot_general(left, right, (((left_dim,), (right_dim,)), ((), ())), pre...]
    unnamed x4, waiting for transfers between devices: 686 us -> 0.07 us
    pallas_call x0 -> x4, Pallas kernels: none -> 323 us  [the longest x2 198 us: mixer_backward(): pl.pallas_call(backward_kernel, grid=(count // MB_TOK, CHUNKS), in_specs=...]
    slice x4, local copies, waits for them, and re-layouts: 311 us -> 14.9 us  [unpack(): pieces.append(flat_weights[offset:offset + amount].reshape(piece_shape))]
    unnamed x449 -> x55, local copies, waits for them, and re-layouts: 286 us -> 24.6 us
    another operation x175 -> x12, local copies, waits for them, and re-layouts: 186 us -> 1.27 us  [the longest x4 0.58 us: segment_masks(): return jnp.stack(columns, axis=1).astype(F32)]
    mul x87 -> x0, other arithmetic: 162 us -> none  [the longest x2 70.6 us: mixer_core(): activated = jax.nn.silu(summed)]
  transfers between devices with their start and end apart: 2 -> 4, of which waited for: 2 -> 3; matrix products, arithmetic and copies ran while one was open for 1% -> 25% of each run, Pallas kernels for 0% -> 8%
where the time goes in v1:
time: 1320 us; the launch traced here: 1290 us
  local copies, waits for them, and re-layouts  516 us (39%)
  Pallas kernels  323 us (24%)
  waiting for transfers between devices  241 us (18%)
  matrix products  171 us (13%)
  other arithmetic  27.9 us (2%)
  between operations  14.7 us (1%)
    concatenate x2, local copies, waits for them, and re-layouts, per_device(): flat = jnp.concatenate([member.reshape(-1) for member in members])  252 us
    pallas_call x2, Pallas kernels, mixer_backward(): pl.pallas_call(backward_kernel, grid=(count // MB_TOK, CHUNKS), in_specs=...  198 us
    reduce_scatter x2, waiting for transfers between devices, per_device(): summed = lax.psum_scatter(rows, 'dp', scatter_dimension=0, tiled=True)  137 us
    dot_general x10, matrix products, dot(): lax.dot_general(left, right, (((left_dim,), (right_dim,)), ((), ())), pre...  136 us
    pallas_call x2, Pallas kernels, mixer_forward(): pl.pallas_call(forward_kernel, grid=(count // MB_TOK, CHUNKS), in_specs=c...  125 us
    all_gather x2, waiting for transfers between devices, per_device(): flat = lax.all_gather(mine, 'dp', axis=0)[:, :shard].reshape(-1)  104 us
    reshape x2, local copies, waits for them, and re-layouts, per_device(): flat.reshape(devices, shard)  37.9 us
    reshape x6, local copies, waits for them, and re-layouts, per_device(): flat = jnp.concatenate([member.reshape(-1) for member in members])  34.7 us
  transfers between devices with their start and end apart: 4, of which 3 were waited for; matrix products, arithmetic and copies ran while one was open for 25% of the time, Pallas kernels for 8%

profile of v1, /device:TPU:0, one launch (start us, length us, event | category | flops | bytes accessed | tf_op | source)
XLA Modules:
  0.0 1293.2 jit_solution(6831118247423281354)
XLA Ops:
  7.2 3.9 slice_reduce_fusion
  12.7 4.6 copy.58
  19.2 4.7 copy.63
  27.1 61.8 %all-gather.5.cloned.1.call-done = bf16[3801088]{0:T(1024)(128)(2,1)} async-done(((bf16[118784]{0:T(1024)(128)(2,1)}), bf16[3801088]{0:T(1024)(128)(2,1)}) %all-gather.5.cloned.1.call-update) | async-done | bytes 7602192 | tf_op jit(solution)/shard_map/all_gather | solution.py:473
  89.0 8.6 reshape.155
  97.6 6.9 slice.174
  104.5 17.1 %reshape.127 = bf16[3765344]{0:T(1024)(128)(2,1)} reshape(bf16[32,117667]{1,0:T(8,128)(2,1)} %slice.174) | data formatting | bytes 15061376 | tf_op jit(solution)/shard_map/reshape | solution.py:473
  123.2 42.1 %all-gather.7.cloned.1.call-done = bf16[3801088]{0:T(1024)(128)(2,1)} async-done(((bf16[118784]{0:T(1024)(128)(2,1)}), bf16[3801088]{0:T(1024)(128)(2,1)}) %all-gather.7.cloned.1.call-update) | async-done | bytes 7602192 | tf_op jit(solution)/shard_map/all_gather | solution.py:473
  165.3 8.2 reshape.156
  173.5 6.6 slice.185
  180.1 17.2 %reshape.132 = bf16[3765344]{0:T(1024)(128)(2,1)} reshape(bf16[32,117667]{1,0:T(8,128)(2,1)} %slice.185) | data formatting | bytes 15061376 | tf_op jit(solution)/shard_map/reshape | solution.py:473
  200.2 6.4 slice.176
  217.6 10.4 reshape.128
  228.1 5.3 reshape.131
  233.5 20.2 %fusion.18.proj_ref.prev_ref = f32[2048,3456]{1,0:T(8,128)} fusion(bf16[768,3352]{1,0:T(8,128)(2,1)} %reshape.128, bf16[2048,768]{0,1:T(8,128)(2,1)} %copy.58, f32[768]{0:T(1024)S(1)} %slice_convert_fusion.7, f32[2048]{0:T(1024)S(1)} %fusion.28), kind=kOutput, calls=%fused_computation.33 | convolution fusion | flops 10877927424 | bytes 36617216 | tf_op jit(solution)/shard_map/dot_general | solution.py:40
  253.9 62.8 %mixer_forward.2 = (bf16[2048,1536]{1,0:T(8,128)(2,1)}, f32[2048,1536]{1,0:T(8,128)}, bf16[16,128,1536]{2,1,0:T(8,128)(2,1)}) custom-call(f32[2048,3456]{1,0:T(8,128)} %fusion.18.proj_ref.prev_ref, f32[2048,3456]{1,0:T(8,128)} %fusion.18.proj_ref.prev_ref, f32[2048,8]{1,0:T(8,128)S(1)} %convert_element_type.78.mask_ref, s32[2048,1]{1,0:T(8,128)S(1)} %copy.60.seg_col_ref, ...), custom_call_target="tpu_custom_call" | custom-call | flops 6291456000 | bytes 62914560 | tf_op jit(solution)/shard_map/mixer_forward/pallas_call | solution.py:348
  316.7 10.4 multiply_reduce_fusion.2
  327.1 10.4 reshape.133
  337.5 5.4 reshape.134
  342.9 10.2 fusion.22.grad_ref
  353.1 19.2 %fusion.14.proj_ref.prev_ref = f32[2048,3456]{1,0:T(8,128)} fusion(bf16[768,3352]{1,0:T(8,128)(2,1)S(1)} %copy-done.12, f32[2048,768]{0,1:T(8,128)} %get-tuple-element.76, f32[768]{0:T(1024)S(1)} %slice_convert_fusion.6, f32[2048]{0:T(1024)S(1)} %fusion.29), kind=kOutput, calls=%fused_computation.29 | convolution fusion | flops 10876354560 | bytes 39762944 | tf_op jit(solution)/shard_map/dot_general | solution.py:40
  372.3 62.5 %mixer_forward.3 = (bf16[2048,1536]{1,0:T(8,128)(2,1)}, f32[2048,1536]{1,0:T(8,128)}, bf16[16,128,1536]{2,1,0:T(8,128)(2,1)}) custom-call(f32[2048,3456]{1,0:T(8,128)} %fusion.14.proj_ref.prev_ref, f32[2048,3456]{1,0:T(8,128)} %fusion.14.proj_ref.prev_ref, f32[2048,8]{1,0:T(8,128)S(1)} %convert_element_type.78.mask_ref, s32[2048,1]{1,0:T(8,128)S(1)} %copy.60.seg_col_ref, ...), custom_call_target="tpu_custom_call" | custom-call | flops 6291456000 | bytes 62914560 | tf_op jit(solution)/shard_map/mixer_forward/pallas_call | solution.py:348
  434.8 99.0 %mixer_backward.2 = (bf16[2048,3456]{1,0:T(8,128)(2,1)}, f32[8,1792]{1,0:T(8,128)S(1)}, f32[8,1536]{1,0:T(8,128)S(1)}, f32[8,128]{1,0:T(8,128)S(1)}) custom-call(f32[2048,3456]{1,0:T(8,128)} %fusion.14.proj_ref.prev_ref, f32[2048,3456]{1,0:T(8,128)} %fusion.14.proj_ref.prev_ref, f32[2048,8]{1,0:T(8,128)S(1)} %convert_element_type.78.mask_ref, ...), custom_call_target="tpu_custom_call" | custom-call | flops 18874368000 | bytes 94371840 | tf_op jit(solution)/shard_map/mixer_backward/pallas_call | solution.py:374
  533.8 17.4 %fusion = f32[768,3352]{1,0:T(8,128)} fusion(bf16[2048,3456]{1,0:T(8,128)(2,1)} %get-tuple-element.23, f32[2048,768]{0,1:T(8,128)S(1)} %bitcast.65, f32[768]{0:T(1024)S(1)} %slice_convert_fusion.6, f32[2048]{0:T(1024)S(1)} %fusion.29), kind=kOutput, calls=%fused_computation | convolution fusion | flops 10549198848 | bytes 30755840 | tf_op jit(solution)/shard_map/slice | solution.py:496
  551.2 18.7 %multiply_reduce_fusion = (f32[768]{0:T(1024)S(1)}, f32[2048]{0:T(1024)S(1)}, f32[2048,768]{0,1:T(8,128)}) fusion(f32[2048,768]{0,1:T(8,128)S(1)} %bitcast.65, f32[2048]{0:T(1024)S(1)} %fusion.29, f32[768]{0:T(1024)S(1)} %slice_convert_fusion.6, bf16[2048,3456]{1,0:T(8,128)(2,1)} %get-tuple-element.23, bf16[768,3352]{1,0:T(8,128)(2,1)} %reshape.133), kind=kOutput, calls=%fused_computation.21 | convolution fusion | flops 10881070080 | bytes 31909888 | tf_op jit(solution)/shard_map/dot_general | solution.py:40
  569.9 11.6 reshape.140
  581.8 9.6 fusion.20
  591.4 5.7 reshape.142
  597.1 126.0 %concatenate.23 = f32[3765344]{0:T(1024)} concatenate(f32[768]{0:T(1024)S(1)} %get-tuple-element.47, f32[2574336]{0:T(1024)} %reshape.140, f32[7168]{0:T(1024)S(1)} %reshape.141, f32[1792]{0:T(1024)S(1)} %slice_reduce_fusion.3, f32[24]{0:T(128)S(1)} %get-tuple-element.68, f32[24]{0:T(128)S(1)} %get-tuple-element.67, f32[24]{0:T(128)S(1)} %reduce_sum.83, ...), dimensions={0} | concatenate | bytes 30122752 | tf_op jit(solution)/shard_map/concatenate | solution.py:512
  723.2 18.9 %reshape.143 = f32[32,117667]{1,0:T(8,128)} reshape(f32[3765344]{0:T(1024)} %concatenate.23) | data formatting | bytes 30122752 | tf_op jit(solution)/shard_map/reshape | solution.py:513
  742.1 11.5 pad.55
  753.6 11.2 reshape.144
  765.4 7.2 convert_add_fusion.1
  775.3 8.7 fusion.24
  783.9 5.7 reshape.137
  789.7 10.7 fusion.25.grad_ref
  800.4 98.8 %mixer_backward.3 = (bf16[2048,3456]{1,0:T(8,128)(2,1)}, f32[8,1792]{1,0:T(8,128)S(1)}, f32[8,1536]{1,0:T(8,128)S(1)}, f32[8,128]{1,0:T(8,128)S(1)}) custom-call(f32[2048,3456]{1,0:T(8,128)} %fusion.18.proj_ref.prev_ref, f32[2048,3456]{1,0:T(8,128)} %fusion.18.proj_ref.prev_ref, f32[2048,8]{1,0:T(8,128)S(1)} %convert_element_type.78.mask_ref, ...), custom_call_target="tpu_custom_call" | custom-call | flops 18874368000 | bytes 94371840 | tf_op jit(solution)/shard_map/mixer_backward/pallas_call | solution.py:374
  899.2 17.3 %fusion.2 = f32[768,3352]{1,0:T(8,128)} fusion(bf16[2048,3456]{1,0:T(8,128)(2,1)} %get-tuple-element.26, bf16[2048,768]{0,1:T(8,128)(2,1)S(1)} %copy-done.9, f32[768]{0:T(1024)S(1)} %copy-done.21, f32[2048]{0:T(1024)S(1)} %copy-done.17), kind=kOutput, calls=%fused_computation.2 | convolution fusion | flops 10550771712 | bytes 27610112 | tf_op jit(solution)/shard_map/slice | solution.py:496
  916.5 11.6 reshape.135
  928.4 19.3 %fusion.7 = (f32[768]{0:T(1024)S(1)}, f32[2048]{0:T(1024)S(1)}, f32[2048,768]{0,1:T(8,128)}) fusion(bf16[2048,768]{0,1:T(8,128)(2,1)} %copy.58, f32[2048]{0:T(1024)S(1)} %copy-done.17, f32[768]{0:T(1024)S(1)} %copy-done.21, bf16[2048,3456]{1,0:T(8,128)(2,1)} %get-tuple-element.26, bf16[768,3352]{1,0:T(8,128)(2,1)} %reshape.128), kind=kOutput, calls=%fused_computation.16 | convolution fusion | flops 10882642944 | bytes 28764160 | tf_op jit(solution)/shard_map/dot_general | solution.py:40
  947.7 125.5 %concatenate.22 = f32[3765344]{0:T(1024)} concatenate(f32[768]{0:T(1024)S(1)} %get-tuple-element.49, f32[2574336]{0:T(1024)} %reshape.135, f32[7168]{0:T(1024)S(1)} %reshape.136, f32[1792]{0:T(1024)S(1)} %slice_reduce_fusion.4, f32[24]{0:T(128)S(1)} %get-tuple-element.70, f32[24]{0:T(128)S(1)} %get-tuple-element.69, f32[24]{0:T(128)S(1)} %reduce_sum.78, ...), dimensions={0} | concatenate | bytes 30122752 | tf_op jit(solution)/shard_map/concatenate | solution.py:512
  1073.3 19.0 %reshape.138 = f32[32,117667]{1,0:T(8,128)} reshape(f32[3765344]{0:T(1024)} %concatenate.22) | data formatting | bytes 30122752 | tf_op jit(solution)/shard_map/reshape | solution.py:513
  1092.2 11.5 pad.54
  1103.7 11.2 reshape.139
  1118.7 8.0 fusion.9
  1126.6 6.6 copy.73
  1133.2 9.2 add_convert_fusion
  1145.2 137.0 %reduce-scatter.5.cloned.1.call-done = f32[928,128]{1,0:T(8,128)} async-done(((f32[29696,128]{1,0:T(8,128)}), f32[928,128]{1,0:T(8,128)}) %reduce-scatter.5.cloned.1.call-update) | async-done | bytes 475152 | tf_op jit(solution)/shard_map/reduce_scatter | solution.py:517
  (135 shorter events, 36.7 us)
Async XLA Ops:
  7.2 10.3 copy-start
  7.2 81.8 %all-gather.5.cloned.1.call-start = ((), (), s32[]{:S(2)}) async-start(), calls=%async_computation.4 | async-start | bytes 7839744 | tf_op jit(solution)/shard_map/all_gather | solution.py:473
  11.8 153.5 %all-gather.7.cloned.1.call-start = ((), (), s32[]{:S(2)}) async-start(), calls=%async_computation.5 | async-start | bytes 7839744 | tf_op jit(solution)/shard_map/all_gather | solution.py:473
  12.6 1102.3 %reduce-scatter.3.cloned.1.call-start = ((), (), s32[]{:S(2)}) async-start(), calls=%async_computation.2 | async-start | bytes 15679488 | tf_op jit(solution)/shard_map/reduce_scatter | solution.py:517
  26.5 0.6 copy-start.14
  27.1 206.3 %copy-start.16 = (f32[2048]{0:T(1024)}, f32[2048]{0:T(1024)S(1)}, u32[]{:S(2)}) copy-start(f32[2048]{0:T(1024)S(1)} %fusion.28) | copy-start | bytes 24580
  197.3 9.9 copy-start.7
  200.2 33.3 %copy-start.20 = (f32[768]{0:T(1024)}, f32[768]{0:T(1024)S(1)}, u32[]{:S(2)}) copy-start(f32[768]{0:T(1024)S(1)} %slice_convert_fusion.7) | copy-start | bytes 9220
  233.5 20.4 %copy-start.5 = (f32[8,128]{1,0:T(8,128)}, f32[8,128]{1,0:T(8,128)S(1)}, u32[]{:S(2)}) copy-start(f32[8,128]{1,0:T(8,128)S(1)} %select_maximum_fusion.1.head_ref) | copy-start | bytes 12292
  253.8 62.9 %copy-start.3 = (f32[8,1536]{1,0:T(8,128)}, f32[8,1536]{1,0:T(8,128)S(1)}, u32[]{:S(2)}) copy-start(f32[8,1536]{1,0:T(8,128)S(1)} %get-tuple-element.72.wide_ref) | copy-start | bytes 147460
  253.9 62.8 %copy-start.1 = (f32[8,1792]{1,0:T(8,128)}, f32[8,1792]{1,0:T(8,128)S(1)}, u32[]{:S(2)}) copy-start(f32[8,1792]{1,0:T(8,128)S(1)} %get-tuple-element.74.conv_ref) | copy-start | bytes 172036
  253.9 62.8 %copy-start.8 = (bf16[2048,768]{0,1:T(8,128)(2,1)S(1)}, bf16[2048,768]{0,1:T(8,128)(2,1)}, u32[]{:S(2)}) copy-start(bf16[2048,768]{0,1:T(8,128)(2,1)} %copy.58) | copy-start | bytes 9437188
  253.9 62.8 %copy-start.13 = (bf16[1536,768]{1,0:T(8,128)(2,1)S(1)}, bf16[1536,768]{1,0:T(8,128)(2,1)}, u32[]{:S(2)}) copy-start(bf16[1536,768]{1,0:T(8,128)(2,1)} %reshape.131) | copy-start | bytes 7077892
  327.1 15.7 %copy-start.18 = (f32[2048]{0:T(1024)}, f32[2048]{0:T(1024)S(1)}, u32[]{:S(2)}) copy-start(f32[2048]{0:T(1024)S(1)} %get-tuple-element.75) | copy-start | bytes 24580
  342.9 10.2 copy-start.12
  372.3 161.5 %slice-start = ((s8[6291456]{0:T(1024)(128)(4,1)}), s8[4194304]{0:T(1024)(128)(4,1)S(1)}, s32[]{:S(2)}) async-start(s8[6291456]{0:T(1024)(128)(4,1)} %bitcast.64), calls=%async_computation.6 | async-start | bytes 8388608
  434.8 99.0 %slice-start.1 = ((s8[6291456]{0:T(1024)(128)(4,1)}), s8[2097152]{0:T(1024)(128)(4,1)S(1)}, s32[]{:S(2)}) async-start(s8[6291456]{0:T(1024)(128)(4,1)} %bitcast.64), calls=%async_computation.7 | async-start | bytes 4194304
  764.7 0.7 copy-start.19
  764.8 517.5 %reduce-scatter.5.cloned.1.call-start = ((), (), s32[]{:S(2)}) async-start(), calls=%async_computation.3 | async-start | bytes 15679488 | tf_op jit(solution)/shard_map/reduce_scatter | solution.py:517
  772.6 2.7 copy-start.11
  789.7 10.7 copy-start.2
  789.7 10.7 copy-start.4
  789.7 10.7 copy-start.6
  800.4 98.8 %copy-start.9 = (bf16[2048,768]{0,1:T(8,128)(2,1)S(1)}, bf16[2048,768]{0,1:T(8,128)(2,1)}, u32[]{:S(2)}) copy-start(bf16[2048,768]{0,1:T(8,128)(2,1)} %copy.58) | copy-start | bytes 9437188
  800.4 98.8 %copy-start.17 = (f32[2048]{0:T(1024)S(1)}, f32[2048]{0:T(1024)}, u32[]{:S(2)}) copy-start(f32[2048]{0:T(1024)} %copy-done.16) | copy-start | bytes 24580
  800.4 98.8 %copy-start.21 = (f32[768]{0:T(1024)S(1)}, f32[768]{0:T(1024)}, u32[]{:S(2)}) copy-start(f32[768]{0:T(1024)} %copy-done.20) | copy-start | bytes 9220
  1116.8 0.7 copy-start.15
  1116.8 1.9 copy-start.10
Sparse Core Ops, SparseCore 0:
  11.9 76.9 all-gather.4
  92.4 72.8 all-gather.6
  764.9 165.2 reduce-scatter.2
  1116.9 165.2 reduce-scatter.4

commit v2 on v1

--- a/solution.py
+++ b/solution.py
@@ -497,19 +497,21 @@
         grad_normed = dot(grad_projected, in_weight, 1, 1)
         stream_part, gain_grad = norm_pull(grad_normed)
         grad_stream = grad_stream + stream_part
-        members = [
-            gain_grad,
-            grad_in_weight,
-            gconv[:4],
-            gconv[4],
-            ghead[0, :HEADS],
-            ghead[1, :HEADS],
-            gwide[0].reshape(HEADS, HEADDIM).sum(axis=1),
-            gwide[1],
-            grad_out_weight,
-            jnp.zeros((shard * devices - PARAMS,), F32),
-        ]
-        flat = jnp.concatenate([member.reshape(-1) for member in members])
+        small_grads = jnp.concatenate(
+            [
+                gconv[:5].reshape(-1),
+                ghead[0, :HEADS],
+                ghead[1, :HEADS],
+                gwide[0].reshape(HEADS, HEADDIM).sum(axis=1),
+                gwide[1],
+            ]
+        )
+        flat = jnp.zeros((shard * devices,), F32)
+        offset = 0
+        for member in (gain_grad, grad_in_weight, small_grads, grad_out_weight):
+            spare = shard * devices - offset - member.size
+            flat = flat + lax.pad(member.reshape(-1), jnp.float32(0.0), ((offset, spare, 0),))
+            offset = offset + member.size
         rows = jnp.pad(flat.reshape(devices, shard), ((0, 0), (0, padded_shard - shard)))
         rows = rows.reshape(-1, LANES)
         if layer + 1 < LAYERS:

time: 1320 us -> 1180 us (0.89); the launches traced: 1290 us -> 1170 us
  local copies, waits for them, and re-layouts: 516 us -> 263 us
  waiting for transfers between devices: 241 us -> 326 us
  other arithmetic: 27.9 us -> 81 us
    concatenate x2, local copies, waits for them, and re-layouts: 252 us -> 0.16 us  [per_device(): jnp.concatenate([gconv[:5].reshape(-1), ghead[0, :HEADS], ghead[1, :HEADS...]
    reduce_scatter x2, waiting for transfers between devices: 137 us -> 224 us  [per_device(): summed = lax.psum_scatter(rows, 'dp', scatter_dimension=0, tiled=True)]
    add x0 -> x2, other arithmetic: none -> 51.7 us  [per_device(): flat + lax.pad(member.reshape(-1), jnp.float32(0.0), ((offset, spare, 0),))]
  transfers between devices with their start and end apart: 4 -> 4, of which waited for: 3 -> 4; matrix products, arithmetic and copies ran while one was open for 25% -> 14% of each run, Pallas kernels for 8% -> 0%
where the time goes in v2:
time: 1180 us; the launch traced here: 1170 us
  waiting for transfers between devices  326 us (28%)
  Pallas kernels  321 us (27%)
  local copies, waits for them, and re-layouts  263 us (22%)
  matrix products  166 us (14%)
  other arithmetic  81 us (7%)
  between operations  14.7 us (1%)
    reduce_scatter x2, waiting for transfers between devices, per_device(): summed = lax.psum_scatter(rows, 'dp', scatter_dimension=0, tiled=True)  224 us
    pallas_call x2, Pallas kernels, mixer_backward(): pl.pallas_call(backward_kernel, grid=(count // MB_TOK, CHUNKS), in_specs=...  196 us
    dot_general x10, matrix products, dot(): lax.dot_general(left, right, (((left_dim,), (right_dim,)), ((), ())), pre...  132 us
    pallas_call x2, Pallas kernels, mixer_forward(): pl.pallas_call(forward_kernel, grid=(count // MB_TOK, CHUNKS), in_specs=c...  125 us
    all_gather x2, waiting for transfers between devices, per_device(): flat = lax.all_gather(mine, 'dp', axis=0)[:, :shard].reshape(-1)  101 us
    add x2, other arithmetic, per_device(): flat + lax.pad(member.reshape(-1), jnp.float32(0.0), ((offset, spare, 0),))  51.7 us
    reshape x2, local copies, waits for them, and re-layouts, per_device(): flat.reshape(devices, shard)  38 us
    reshape x4, local copies, waits for them, and re-layouts, per_device(): member.reshape(-1)  34.7 us
  transfers between devices with their start and end apart: 4, of which 4 were waited for; matrix products, arithmetic and copies ran while one was open for 14% of the time, Pallas kernels for 0%

profile of v2, /device:TPU:0, one launch (start us, length us, event | category | flops | bytes accessed | tf_op | source)
XLA Modules:
  0.0 1172.5 jit_solution(4091106312293871747)
XLA Ops:
  17.4 4.7 copy.58
  22.1 4.7 copy.63
  29.9 59.1 %all-gather.7.cloned.1.call-done = bf16[3801088]{0:T(1024)(128)(2,1)} async-done(((bf16[118784]{0:T(1024)(128)(2,1)}), bf16[3801088]{0:T(1024)(128)(2,1)}) %all-gather.7.cloned.1.call-update) | async-done | bytes 7602192 | tf_op jit(solution)/shard_map/all_gather | solution.py:473
  89.0 8.3 reshape.156
  97.3 6.9 slice.177
  104.2 17.1 %reshape.132 = bf16[3765344]{0:T(1024)(128)(2,1)} reshape(bf16[32,117667]{1,0:T(8,128)(2,1)} %slice.177) | data formatting | bytes 15061376 | tf_op jit(solution)/shard_map/reshape | solution.py:473
  122.8 42.4 %all-gather.5.cloned.1.call-done = bf16[3801088]{0:T(1024)(128)(2,1)} async-done(((bf16[118784]{0:T(1024)(128)(2,1)}), bf16[3801088]{0:T(1024)(128)(2,1)}) %all-gather.5.cloned.1.call-update) | async-done | bytes 7602192 | tf_op jit(solution)/shard_map/all_gather | solution.py:473
  165.3 8.5 reshape.155
  173.8 6.6 slice.166
  180.4 17.2 %reshape.127 = bf16[3765344]{0:T(1024)(128)(2,1)} reshape(bf16[32,117667]{1,0:T(8,128)(2,1)} %slice.166) | data formatting | bytes 15061376 | tf_op jit(solution)/shard_map/reshape | solution.py:473
  208.5 6.3 slice.168
  220.6 5.4 reshape.131
  225.9 10.4 reshape.128
  236.3 5.3 reshape.134
  241.7 10.4 reshape.133
  252.1 20.2 %fusion.18.proj_ref.prev_ref = f32[2048,3456]{1,0:T(8,128)} fusion(bf16[768,3352]{1,0:T(8,128)(2,1)} %reshape.128, bf16[2048,768]{0,1:T(8,128)(2,1)} %copy.58, f32[768]{0:T(1024)S(1)} %slice_convert_fusion.7, f32[2048]{0:T(1024)S(1)} %fusion.28), kind=kOutput, calls=%fused_computation.35 | convolution fusion | flops 10877927424 | bytes 36617216 | tf_op jit(solution)/shard_map/dot_general | solution.py:40
  272.6 62.4 %mixer_forward.2 = (bf16[2048,1536]{1,0:T(8,128)(2,1)}, f32[2048,1536]{1,0:T(8,128)}, bf16[16,128,1536]{2,1,0:T(8,128)(2,1)}) custom-call(f32[2048,3456]{1,0:T(8,128)} %fusion.18.proj_ref.prev_ref, f32[2048,3456]{1,0:T(8,128)} %fusion.18.proj_ref.prev_ref, f32[2048,8]{1,0:T(8,128)S(1)} %convert_element_type.78.mask_ref, s32[2048,1]{1,0:T(8,128)S(1)} %copy.60.seg_col_ref, ...), custom_call_target="tpu_custom_call" | custom-call | flops 6291456000 | bytes 62914560 | tf_op jit(solution)/shard_map/mixer_forward/pallas_call | solution.py:348
  335.0 8.6 multiply_reduce_fusion.2
  343.7 8.2 fusion.22.grad_ref
  351.9 18.0 %fusion.14.proj_ref.prev_ref = f32[2048,3456]{1,0:T(8,128)} fusion(bf16[768,3352]{1,0:T(8,128)(2,1)} %reshape.133, f32[2048,768]{0,1:T(8,128)S(1)} %get-tuple-element.76, f32[768]{0:T(1024)S(1)} %slice_convert_fusion.6, f32[2048]{0:T(1024)S(1)} %fusion.29), kind=kOutput, calls=%fused_computation.31 | convolution fusion | flops 10876354560 | bytes 39762944 | tf_op jit(solution)/shard_map/dot_general | solution.py:40
  369.8 62.6 %mixer_forward.3 = (bf16[2048,1536]{1,0:T(8,128)(2,1)}, f32[2048,1536]{1,0:T(8,128)}, bf16[16,128,1536]{2,1,0:T(8,128)(2,1)}) custom-call(f32[2048,3456]{1,0:T(8,128)} %fusion.14.proj_ref.prev_ref, f32[2048,3456]{1,0:T(8,128)} %fusion.14.proj_ref.prev_ref, f32[2048,8]{1,0:T(8,128)S(1)} %convert_element_type.78.mask_ref, s32[2048,1]{1,0:T(8,128)S(1)} %copy.60.seg_col_ref, ...), custom_call_target="tpu_custom_call" | custom-call | flops 6291456000 | bytes 62914560 | tf_op jit(solution)/shard_map/mixer_forward/pallas_call | solution.py:348
  432.4 98.1 %mixer_backward.2 = (bf16[2048,3456]{1,0:T(8,128)(2,1)}, f32[8,1792]{1,0:T(8,128)S(1)}, f32[8,1536]{1,0:T(8,128)S(1)}, f32[8,128]{1,0:T(8,128)S(1)}) custom-call(f32[2048,3456]{1,0:T(8,128)} %fusion.14.proj_ref.prev_ref, f32[2048,3456]{1,0:T(8,128)} %fusion.14.proj_ref.prev_ref, f32[2048,8]{1,0:T(8,128)S(1)} %convert_element_type.78.mask_ref, ...), custom_call_target="tpu_custom_call" | custom-call | flops 18874368000 | bytes 94371840 | tf_op jit(solution)/shard_map/mixer_backward/pallas_call | solution.py:374
  530.5 18.5 %multiply_reduce_fusion = (f32[768]{0:T(1024)S(1)}, f32[2048]{0:T(1024)S(1)}, f32[2048,768]{0,1:T(8,128)}) fusion(f32[2048,768]{0,1:T(8,128)S(1)} %get-tuple-element.76, f32[2048]{0:T(1024)S(1)} %fusion.29, f32[768]{0:T(1024)S(1)} %slice_convert_fusion.6, bf16[2048,3456]{1,0:T(8,128)(2,1)} %get-tuple-element.23, bf16[768,3352]{1,0:T(8,128)(2,1)} %reshape.133), kind=kOutput, calls=%fused_computation.23 | convolution fusion | flops 10881070080 | bytes 31909888 | tf_op jit(solution)/shard_map/dot_general | solution.py:40
  549.1 17.4 %fusion = f32[768,3352]{1,0:T(8,128)} fusion(bf16[2048,3456]{1,0:T(8,128)(2,1)} %get-tuple-element.23, f32[2048,768]{0,1:T(8,128)S(1)} %get-tuple-element.76, f32[768]{0:T(1024)S(1)} %slice_convert_fusion.6, f32[2048]{0:T(1024)S(1)} %fusion.29), kind=kOutput, calls=%fused_computation.2 | convolution fusion | flops 10549198848 | bytes 30755840 | tf_op jit(solution)/shard_map/slice | solution.py:496
  566.5 5.7 convert_add_fusion.1
  572.2 11.0 fusion.24
  583.2 8.5 fusion.25.grad_ref
  591.7 98.4 %mixer_backward.3 = (bf16[2048,3456]{1,0:T(8,128)(2,1)}, f32[8,1792]{1,0:T(8,128)S(1)}, f32[8,1536]{1,0:T(8,128)S(1)}, f32[8,128]{1,0:T(8,128)S(1)}) custom-call(f32[2048,3456]{1,0:T(8,128)} %fusion.18.proj_ref.prev_ref, f32[2048,3456]{1,0:T(8,128)} %fusion.18.proj_ref.prev_ref, f32[2048,8]{1,0:T(8,128)S(1)} %convert_element_type.78.mask_ref, ...), custom_call_target="tpu_custom_call" | custom-call | flops 18874368000 | bytes 94371840 | tf_op jit(solution)/shard_map/mixer_backward/pallas_call | solution.py:374
  690.1 18.9 %fusion.7 = (f32[768]{0:T(1024)S(1)}, f32[2048]{0:T(1024)S(1)}, f32[2048,768]{0,1:T(8,128)}) fusion(bf16[2048,768]{0,1:T(8,128)(2,1)S(1)} %copy-done.8, f32[2048]{0:T(1024)S(1)} %copy-done.18, f32[768]{0:T(1024)S(1)} %copy-done.20, bf16[2048,3456]{1,0:T(8,128)(2,1)} %get-tuple-element.26, bf16[768,3352]{1,0:T(8,128)(2,1)} %reshape.128), kind=kOutput, calls=%fused_computation.18 | convolution fusion | flops 10882642944 | bytes 28764160 | tf_op jit(solution)/shard_map/dot_general | solution.py:40
  709.0 17.2 %fusion.2 = f32[768,3352]{1,0:T(8,128)} fusion(bf16[2048,3456]{1,0:T(8,128)(2,1)} %get-tuple-element.26, bf16[2048,768]{0,1:T(8,128)(2,1)S(1)} %copy-done.8, f32[768]{0:T(1024)S(1)} %copy-done.20, f32[2048]{0:T(1024)S(1)} %copy-done.18), kind=kOutput, calls=%fused_computation.4 | convolution fusion | flops 10550771712 | bytes 27610112 | tf_op jit(solution)/shard_map/slice | solution.py:496
  726.4 9.6 fusion.20
  736.0 5.7 reshape.142
  741.7 11.6 reshape.140
  753.3 5.7 reshape.137
  759.1 25.8 %pad_add_fusion = f32[3765344]{0:T(1024)} fusion(f32[1179648]{0:T(1024)} %reshape.142, f32[10568]{0:T(1024)S(1)} %concatenate.23, f32[2574336]{0:T(1024)} %reshape.140, f32[768]{0:T(1024)S(1)} %get-tuple-element.47), kind=kLoop, calls=%fused_computation | loop fusion | flops 11296032 | bytes 30122656 | tf_op jit(solution)/shard_map/add | solution.py:513
  785.0 18.9 %reshape.143 = f32[32,117667]{1,0:T(8,128)} reshape(f32[3765344]{0:T(1024)} %pad_add_fusion) | data formatting | bytes 30122752 | tf_op jit(solution)/shard_map/reshape | solution.py:515
  803.9 11.6 pad.87
  815.5 11.4 reshape.144
  827.2 11.7 %reshape.135 = f32[2574336]{0:T(1024)} reshape(f32[768,3352]{1,0:T(8,128)} %fusion.2) | data formatting | bytes 20594688 | tf_op jit(solution)/shard_map/reshape | solution.py:513
  839.0 25.9 %pad_add_fusion.1 = f32[3765344]{0:T(1024)} fusion(f32[1179648]{0:T(1024)} %reshape.137, f32[10568]{0:T(1024)S(1)} %concatenate.22, f32[2574336]{0:T(1024)} %reshape.135, f32[768]{0:T(1024)S(1)} %get-tuple-element.49), kind=kLoop, calls=%fused_computation.1 | loop fusion | flops 11296032 | bytes 30122656 | tf_op jit(solution)/shard_map/add | solution.py:513
  864.9 19.1 %reshape.138 = f32[32,117667]{1,0:T(8,128)} reshape(f32[3765344]{0:T(1024)} %pad_add_fusion.1) | data formatting | bytes 30122752 | tf_op jit(solution)/shard_map/reshape | solution.py:515
  884.0 11.7 pad.82
  895.6 11.3 reshape.139
  907.0 85.4 %reduce-scatter.3.cloned.1.call-done = f32[928,128]{1,0:T(8,128)} async-done(((f32[29696,128]{1,0:T(8,128)}), f32[928,128]{1,0:T(8,128)}) %reduce-scatter.3.cloned.1.call-update) | async-done | bytes 475152 | tf_op jit(solution)/shard_map/reduce_scatter | solution.py:519
  993.4 10.1 add_convert_fusion
  1008.1 9.0 fusion.9
  1017.1 6.6 copy.73
  1023.7 138.9 %reduce-scatter.5.cloned.1.call-done = f32[928,128]{1,0:T(8,128)} async-done(((f32[29696,128]{1,0:T(8,128)}), f32[928,128]{1,0:T(8,128)}) %reduce-scatter.5.cloned.1.call-update) | async-done | bytes 475152 | tf_op jit(solution)/shard_map/reduce_scatter | solution.py:519
  (130 shorter events, 40.9 us)
Async XLA Ops:
  7.2 81.8 %all-gather.7.cloned.1.call-start = ((), (), s32[]{:S(2)}) async-start(), calls=%async_computation.5 | async-start | bytes 7839744 | tf_op jit(solution)/shard_map/all_gather | solution.py:473
  11.8 153.5 %all-gather.5.cloned.1.call-start = ((), (), s32[]{:S(2)}) async-start(), calls=%async_computation.4 | async-start | bytes 7839744 | tf_op jit(solution)/shard_map/all_gather | solution.py:473
  12.6 979.7 %reduce-scatter.3.cloned.1.call-start = ((), (), s32[]{:S(2)}) async-start(), calls=%async_computation.2 | async-start | bytes 15679488 | tf_op jit(solution)/shard_map/reduce_scatter | solution.py:519
  29.3 0.6 copy-start.15
  29.9 222.2 %copy-start.17 = (f32[2048]{0:T(1024)}, f32[2048]{0:T(1024)S(1)}, u32[]{:S(2)}) copy-start(f32[2048]{0:T(1024)S(1)} %fusion.28) | copy-start | bytes 24580
  199.9 52.2 %copy-start.19 = (f32[768]{0:T(1024)}, f32[768]{0:T(1024)S(1)}, u32[]{:S(2)}) copy-start(f32[768]{0:T(1024)S(1)} %slice_convert_fusion.7) | copy-start | bytes 9220
  204.9 10.0 slice-start
  208.5 6.3 slice-start.1
  252.1 20.4 %copy-start.5 = (f32[8,128]{1,0:T(8,128)}, f32[8,128]{1,0:T(8,128)S(1)}, u32[]{:S(2)}) copy-start(f32[8,128]{1,0:T(8,128)S(1)} %select_maximum_fusion.1.head_ref) | copy-start | bytes 12292
  252.1 20.4 %copy-start = (s32[2048]{0:T(1024)S(1)}, s32[2048]{0:T(1024)}, u32[]{:S(2)}) copy-start(s32[2048]{0:T(1024)} %param.6) | copy-start | bytes 24580
  272.4 62.5 %copy-start.1 = (f32[8,1792]{1,0:T(8,128)}, f32[8,1792]{1,0:T(8,128)S(1)}, u32[]{:S(2)}) copy-start(f32[8,1792]{1,0:T(8,128)S(1)} %get-tuple-element.74.conv_ref) | copy-start | bytes 172036
  272.5 62.4 %copy-start.3 = (f32[8,1536]{1,0:T(8,128)}, f32[8,1536]{1,0:T(8,128)S(1)}, u32[]{:S(2)}) copy-start(f32[8,1536]{1,0:T(8,128)S(1)} %get-tuple-element.72.wide_ref) | copy-start | bytes 147460
  272.6 62.4 %copy-start.7 = (bf16[2048,768]{0,1:T(8,128)(2,1)S(1)}, bf16[2048,768]{0,1:T(8,128)(2,1)}, u32[]{:S(2)}) copy-start(bf16[2048,768]{0,1:T(8,128)(2,1)} %copy.58) | copy-start | bytes 9437188
  335.0 8.7 copy-start.10
  335.0 8.7 copy-start.13
  343.7 205.4 %copy-start.12 = (f32[2048,768]{0,1:T(8,128)}, f32[2048,768]{0,1:T(8,128)S(1)}, u32[]{:S(2)}) copy-start(f32[2048,768]{0,1:T(8,128)S(1)} %get-tuple-element.76) | copy-start | bytes 18874372
  549.1 17.4 %copy-start.11 = (bf16[2048,768]{0,1:T(8,128)(2,1)S(1)}, bf16[2048,768]{0,1:T(8,128)(2,1)}, u32[]{:S(2)}) copy-start(bf16[2048,768]{0,1:T(8,128)(2,1)} %copy.63) | copy-start | bytes 9437188
  572.2 11.0 copy-start.9
  572.2 11.0 copy-start.14
  583.2 8.5 copy-start.2
  583.2 8.5 copy-start.4
  583.2 8.5 copy-start.6
  591.7 98.4 %copy-start.8 = (bf16[2048,768]{0,1:T(8,128)(2,1)S(1)}, bf16[2048,768]{0,1:T(8,128)(2,1)}, u32[]{:S(2)}) copy-start(bf16[2048,768]{0,1:T(8,128)(2,1)} %copy.58) | copy-start | bytes 9437188
  591.7 98.4 %copy-start.18 = (f32[2048]{0:T(1024)S(1)}, f32[2048]{0:T(1024)}, u32[]{:S(2)}) copy-start(f32[2048]{0:T(1024)} %copy-done.17) | copy-start | bytes 24580
  591.7 98.4 %copy-start.20 = (f32[768]{0:T(1024)S(1)}, f32[768]{0:T(1024)}, u32[]{:S(2)}) copy-start(f32[768]{0:T(1024)} %copy-done.19) | copy-start | bytes 9220
  826.9 335.7 %reduce-scatter.5.cloned.1.call-start = ((), (), s32[]{:S(2)}) async-start(), calls=%async_computation.3 | async-start | bytes 15679488 | tf_op jit(solution)/shard_map/reduce_scatter | solution.py:519
  1003.5 4.6 copy-start.16
Sparse Core Ops, SparseCore 0:
  11.9 76.9 all-gather.6
  92.4 72.8 all-gather.4
  827.0 165.2 reduce-scatter.2
  994.6 168.0 reduce-scatter.4
